TPU v7x, 32 devices: a whole 2x2x4 slice. The times are simulated.
32 devices in a mesh: groups: 2 (over y), fsdp: 8 (over z, x), tensor: 2 (over core).
Axes of the slice: x: 2, y: 2, z: 4, core: 2. Of those that a mesh axis runs over, the one named last changes fastest.
Arguments:
- token_ids: int32 [4, 64], P(None, 'groups'), parts along dimension 1, may hold values from 0 to 76031
- embed_table: bfloat16 [5120, 76032], P(('fsdp', 'tensor')), may hold values from -9 to 9
- norm_gain: bfloat16 [5120], replicated, may hold values from 0.099609375 to 1.8984375
- gate_base: bfloat16 [12800, 5120], P(('fsdp', 'tensor')), may hold values from -0.078125 to 0.078125
- up_base: bfloat16 [12800, 5120], P(('fsdp', 'tensor')), may hold values from -0.078125 to 0.078125
- down_base: bfloat16 [12800, 5120], P(('fsdp', 'tensor')), may hold values from -0.078125 to 0.078125
- gate_up_b: bfloat16 [5120, 128], P('fsdp'), may hold values from -0.078125 to 0.078125
- gate_up_a: bfloat16 [128, 12800], P(None, 'fsdp'), may hold values from -0.75 to 0.75
- down_b: bfloat16 [12800, 64], P('fsdp'), may hold values from -0.0546875 to 0.0546875
- down_a: bfloat16 [64, 5120], P(None, 'fsdp'), may hold values from -0.75 to 0.75
Outputs:
- final_stream: bfloat16 [64, 5120], P('groups', ('fsdp', 'tensor')), parts along dimension 0
There are 2 independent parts, one for each index of `groups`. A program takes and returns all parts, laid end to end along the dimension named above; an argument that names none is the same for every part. Nothing has to cross between parts.
All inputs are finite; a program needn't handle non-finite values.
Results may differ from a plain program's by a relative error of at most 0.012.
Values may be sent and summed in bfloat16 or wider, within the bound.
A program may use at most 256 MiB of HBM per device.

v0:
```python
import jax
import jax.numpy as jnp
from jax import lax
from jax.sharding import PartitionSpec as P

epsilon = 1e-06


def on_device(
    token_ids,
    embed_table,
    norm_gain,
    gate_base,
    up_base,
    down_base,
    gate_up_b,
    gate_up_a,
    down_b,
    down_a,
):
    tensor_slot = lax.axis_index("tensor")
    column_slot = lax.axis_index("fsdp") * lax.axis_size("tensor") + tensor_slot
    hidden_dev = gate_base.shape[0]
    columns_dev = embed_table.shape[0]
    rank_size = down_a.shape[0]
    model_width = gate_base.shape[1]
    rows_count = token_ids.shape[1]
    step_count = token_ids.shape[0]
    contract = (((0,), (1,)), ((), ()))
    narrow_local = lax.dynamic_slice_in_dim(gate_up_a, tensor_slot * hidden_dev, hidden_dev, 1)
    down_local = lax.dynamic_slice_in_dim(down_b, tensor_slot * hidden_dev, hidden_dev, 0)
    portion = lax.all_gather(gate_up_b, "fsdp", axis=0, tiled=True)
    gate_part = gate_base.astype(jnp.float32)
    up_part = up_base.astype(jnp.float32)
    gate_fix = lax.dot_general(
        narrow_local[:rank_size],
        portion[:, :rank_size],
        contract,
        preferred_element_type=jnp.float32,
    )
    up_fix = lax.dot_general(
        narrow_local[rank_size:],
        portion[:, rank_size:],
        contract,
        preferred_element_type=jnp.float32,
    )
    merged_inputs = jnp.concatenate(
        [(gate_part + gate_fix).astype(jnp.bfloat16), (up_part + up_fix).astype(jnp.bfloat16)],
        axis=0,
    )
    base_part = down_base.astype(jnp.float32)
    down_fix = jnp.dot(
        down_local,
        lax.all_gather(down_a, "fsdp", axis=1, tiled=True),
        preferred_element_type=jnp.float32,
    )
    merged_down = (base_part + down_fix).astype(jnp.bfloat16)
    looked_local = jnp.transpose(jnp.take(embed_table, token_ids, axis=1), (1, 2, 0))
    looked = lax.all_gather(looked_local, ("fsdp", "tensor"), axis=2, tiled=True)
    gain_value = norm_gain.astype(jnp.float32)
    stream = jnp.zeros((rows_count, model_width), jnp.float32)
    for position in range(step_count):
        stream = stream + looked[position].astype(jnp.float32)
        inverse_rms = lax.rsqrt(jnp.mean(stream * stream, axis=1, keepdims=True) + epsilon)
        normed = (stream * inverse_rms * gain_value).astype(jnp.bfloat16)
        preact = lax.dot_general(
            normed, merged_inputs, (((1,), (1,)), ((), ())), preferred_element_type=jnp.float32
        )
        activated = (jax.nn.silu(preact[:, :hidden_dev]) * preact[:, hidden_dev:]).astype(
            jnp.bfloat16
        )
        stream = stream + lax.psum(
            jnp.dot(activated, merged_down, preferred_element_type=jnp.float32), ("fsdp", "tensor")
        )
    result = lax.dynamic_slice_in_dim(stream, column_slot * columns_dev, columns_dev, 1)
    return result.astype(jnp.bfloat16)


def solution(mesh):
    in_specs = (
        P(None, "groups"),
        P(("fsdp", "tensor"), None),
        P(),
        P(("fsdp", "tensor"), None),
        P(("fsdp", "tensor"), None),
        P(("fsdp", "tensor"), None),
        P("fsdp", None),
        P(None, "fsdp"),
        P("fsdp", None),
        P(None, "fsdp"),
    )
    out_specs = P("groups", ("fsdp", "tensor"))
    return jax.shard_map(
        on_device, mesh=mesh, in_specs=in_specs, out_specs=out_specs, check_vma=False
    )
```

profile of v0, /device:TPU:0, one launch (start us, length us, event | category | flops | bytes accessed | tf_op | source)
XLA Modules:
  0.0 592.8 jit_solution(4740071688076784565)
XLA Ops:
  7.3 65.3 %copy.12 = bf16[320,76032]{0,1:T(8,128)(2,1)} copy(bf16[320,76032]{1,0:T(8,128)(2,1)} %param.11) | data formatting | bytes 97320960 | tf_op args[1]
  72.8 1.9 gather_fusion
  75.9 34.3 %all_gather.11 = bf16[64,5120]{1,0:T(8,128)(2,1)S(1)} all-gather(bf16[64,640]{1,0:T(8,128)(2,1)S(1)} %copy-done.4), channel_id=1, replica_groups=mesh['groups'=2,'fsdp'=8,'tensor'=2] {'fsdp'}, dimensions={1}, use_global_device_ids=true | all-gather | bytes 737280 | tf_op jit(solution)/shard_map/all_gather | solution.py:54
  110.2 8.9 %add_convert_fusion = bf16[800,5120]{1,0:T(8,128)(2,1)} fusion(bf16[800,5120]{1,0:T(8,128)(2,1)} %param.15, bf16[64,5120]{1,0:T(8,128)(2,1)S(1)} %all_gather.11, bf16[1600,64]{0,1:T(8,128)(2,1)S(1)} %copy-done.5, s32[]{:T(128)S(6)} %select_n.23), kind=kOutput, calls=%fused_computation.2 | convolution fusion | flops 536576000 | bytes 17154052 | tf_op jit(solution)/shard_map/dot_general | solution.py:52
  119.1 9.3 %add_convert_fusion.2 = bf16[800,5120]{1,0:T(8,128)(2,1)} fusion(bf16[800,5120]{1,0:T(8,128)(2,1)} %param.13, bf16[5120,128]{1,0:T(8,128)(2,1)} %all-gather.5.cloned.1.call-done, bf16[128,1600]{0,1:T(8,128)(2,1)S(1)} %copy-done, s32[]{:T(128)S(6)} %select_n.23), kind=kOutput, calls=%fused_computation.4 | convolution fusion | flops 536576000 | bytes 17899524 | tf_op jit(solution)/shard_map/dot_general | solution.py:35
  128.4 8.9 %add_convert_fusion.1 = bf16[800,5120]{1,0:T(8,128)(2,1)} fusion(bf16[800,5120]{1,0:T(8,128)(2,1)} %param.14, bf16[5120,128]{1,0:T(8,128)(2,1)S(1)} %copy-done.2, bf16[128,1600]{0,1:T(8,128)(2,1)S(1)} %copy-done, s32[]{:T(128)S(6)} %add.124, s32[]{:T(128)S(6)} %select_n.23), kind=kOutput, calls=%fused_computation.3 | convolution fusion | flops 536576000 | bytes 17899528 | tf_op jit(solution)/shard_map/dot_general | solution.py:41
  138.0 17.8 %fusion.47 = (bf16[1,32,5120]{1,0,2:T(2,128)(2,1)}, bf16[1,32,5120]{1,0,2:T(2,128)(2,1)}, bf16[1,32,5120]{1,0,2:T(2,128)(2,1)}, bf16[1,32,5120]{1,0,2:T(2,128)(2,1)S(1)}) fusion(bf16[4,32,5120]{1,0,2:T(4,128)(2,1)} %all-gather.3.cloned.1.call-done), kind=kLoop, calls=%fused_computation.70 | loop fusion | bytes 2621440 | tf_op jit(solution)/shard_map/slice | solution.py:63
  155.8 4.7 copy.18
  160.7 8.4 %fusion.9 = f32[32,1600]{1,0:T(8,128)S(1)} fusion(bf16[1,32,5120]{2,1,0:T(8,128)(2,1)S(1)} %copy.18, f32[5120]{0:T(1024)S(1)} %convert_element_type.74, f32[32]{0:T(128)S(1)} %add_rsqrt_fusion.3, bf16[800,5120]{1,0:T(8,128)(2,1)} %add_convert_fusion.1, bf16[800,5120]{1,0:T(8,128)(2,1)} %add_convert_fusion.2), kind=kOutput, calls=%fused_computation.25 | convolution fusion | flops 557711360 | bytes 16937088 | tf_op jit(solution)/shard_map/dot_general | solution.py:66
  169.1 5.8 fusion.27
  175.2 4.7 copy.19
  179.9 86.8 %all-reduce.5.cloned.1.call-done = f32[32,5120]{1,0:T(8,128)} async-done(((f32[32,5120]{1,0:T(8,128)}), f32[32,5120]{1,0:T(8,128)}) %all-reduce.5.cloned.1.call-update) | async-done | bytes 655376 | tf_op jit(solution)/shard_map/psum | solution.py:72
  268.0 8.5 %fusion.6 = f32[32,1600]{1,0:T(8,128)S(1)} fusion(f32[32]{0:T(128)S(1)} %add_rsqrt_fusion.2, f32[5120]{0:T(1024)S(1)} %convert_element_type.74, f32[32,5120]{1,0:T(8,128)} %all-reduce.5.cloned.1.call-done, bf16[1,32,5120]{2,1,0:T(8,128)(2,1)S(1)} %copy.19, bf16[1,32,5120]{2,1,0:T(8,128)(2,1)S(1)} %copy.18, bf16[800,5120]{1,0:T(8,128)(2,1)} %add_convert_fusion.1, ...), kind=kOutput, calls=%fused_computation.22 | convolution fusion | flops 558202880 | bytes 17920128 | tf_op jit(solution)/shard_map/dot_general | solution.py:66
  276.5 5.8 fusion.29
  282.4 5.8 copy.20
  288.2 85.2 %all-reduce.7.cloned.1.call-done = f32[32,5120]{1,0:T(8,128)} async-done(((f32[32,5120]{1,0:T(8,128)}), f32[32,5120]{1,0:T(8,128)}) %all-reduce.7.cloned.1.call-update) | async-done | bytes 655376 | tf_op jit(solution)/shard_map/psum | solution.py:72
  373.4 1.8 multiply_reduce_fusion.1
  375.3 8.7 %fusion.7 = f32[32,1600]{1,0:T(8,128)S(1)} fusion(f32[32,5120]{1,0:T(8,128)S(1)} %get-tuple-element.8, f32[32]{0:T(128)S(1)} %add_rsqrt_fusion.1, f32[5120]{0:T(1024)S(1)} %convert_element_type.74, bf16[800,5120]{1,0:T(8,128)(2,1)} %add_convert_fusion.1, bf16[800,5120]{1,0:T(8,128)(2,1)} %add_convert_fusion.2), kind=kOutput, calls=%fused_computation.23 | convolution fusion | flops 557547520 | bytes 17264768 | tf_op jit(solution)/shard_map/dot_general | solution.py:66
  384.0 2.5 fusion.31
  387.9 89.6 %all-reduce.9.cloned.1.call-done = f32[32,5120]{1,0:T(8,128)} async-done(((f32[32,5120]{1,0:T(8,128)}), f32[32,5120]{1,0:T(8,128)}) %all-reduce.9.cloned.1.call-update) | async-done | bytes 655376 | tf_op jit(solution)/shard_map/psum | solution.py:72
  479.0 8.4 %fusion.8 = f32[32,1600]{1,0:T(8,128)S(1)} fusion(f32[32,5120]{1,0:T(8,128)S(1)} %get-tuple-element.6, f32[32]{0:T(128)S(1)} %add_rsqrt_fusion, f32[5120]{0:T(1024)S(1)} %convert_element_type.74, bf16[800,5120]{1,0:T(8,128)(2,1)} %add_convert_fusion.1, bf16[800,5120]{1,0:T(8,128)(2,1)} %add_convert_fusion.2), kind=kOutput, calls=%fused_computation.24 | convolution fusion | flops 557547520 | bytes 17264768 | tf_op jit(solution)/shard_map/dot_general | solution.py:66
  487.5 5.8 fusion.33
  493.3 91.0 %all-reduce.11.cloned.1.call-done = f32[32,5120]{1,0:T(8,128)} async-done(((f32[32,5120]{1,0:T(8,128)}), f32[32,5120]{1,0:T(8,128)}) %all-reduce.11.cloned.1.call-update) | async-done | bytes 655376 | tf_op jit(solution)/shard_map/psum | solution.py:72
  584.4 1.5 fusion.39
  (50 shorter events, 7.6 us)
Async XLA Ops:
  6.5 112.6 %copy-start = (bf16[128,1600]{0,1:T(8,128)(2,1)S(1)}, bf16[128,1600]{0,1:T(8,128)(2,1)}, u32[]{:S(2)}) copy-start(bf16[128,1600]{0,1:T(8,128)(2,1)} %param.17) | copy-start | bytes 1228804
  6.5 112.5 %all-gather.5.cloned.1.call-start = ((), (), s32[]{:S(2)}) async-start(), calls=%async_computation.1 | async-start | bytes 1474560 | tf_op jit(solution)/shard_map/all_gather | solution.py:32
  7.3 65.4 %copy-start.7 = (s32[4,32]{1,0:T(4,128)S(1)}, s32[4,32]{1,0:T(4,128)}, u32[]{:S(2)}) copy-start(s32[4,32]{1,0:T(4,128)} %param.10) | copy-start | bytes 1540
  7.3 68.6 %copy-start.6 = (bf16[5120]{0:T(1024)(128)(2,1)S(1)}, bf16[5120]{0:T(1024)(128)(2,1)}, u32[]{:S(2)}) copy-start(bf16[5120]{0:T(1024)(128)(2,1)} %param.12) | copy-start | bytes 30724
  7.3 68.6 %copy-start.4 = (bf16[64,640]{1,0:T(8,128)(2,1)S(1)}, bf16[64,640]{1,0:T(8,128)(2,1)}, u32[]{:S(2)}) copy-start(bf16[64,640]{1,0:T(8,128)(2,1)} %param.19) | copy-start | bytes 245764
  7.3 102.9 %copy-start.5 = (bf16[1600,64]{0,1:T(8,128)(2,1)S(1)}, bf16[1600,64]{0,1:T(8,128)(2,1)}, u32[]{:S(2)}) copy-start(bf16[1600,64]{0,1:T(8,128)(2,1)} %param.18) | copy-start | bytes 614404
  7.3 130.7 %all-gather.3.cloned.1.call-start = ((), (), s32[]{:S(2)}) async-start(), calls=%async_computation | async-start | bytes 5570560 | tf_op jit(solution)/shard_map/all_gather | solution.py:59
  75.8 190.9 %all-reduce.5.cloned.1.call-start = ((), (), s32[]{:S(2)}) async-start(), calls=%async_computation.2 | async-start | bytes 1310720 | tf_op jit(solution)/shard_map/psum | solution.py:72
  119.1 9.3 %copy-start.2 = (bf16[5120,128]{1,0:T(8,128)(2,1)S(1)}, bf16[5120,128]{1,0:T(8,128)(2,1)}, u32[]{:S(2)}) copy-start(bf16[5120,128]{1,0:T(8,128)(2,1)} %all-gather.5.cloned.1.call-done) | copy-start | bytes 3932164
  175.0 198.4 %all-reduce.7.cloned.1.call-start = ((), (), s32[]{:S(2)}) async-start(), calls=%async_computation.3 | async-start | bytes 1310720 | tf_op jit(solution)/shard_map/psum | solution.py:72
  282.4 195.1 %all-reduce.9.cloned.1.call-start = ((), (), s32[]{:S(2)}) async-start(), calls=%async_computation.4 | async-start | bytes 1310720 | tf_op jit(solution)/shard_map/psum | solution.py:72
  373.4 10.5 %slice-start = ((s8[8192000]{0:T(1024)(128)(4,1)}), s8[4194304]{0:T(1024)(128)(4,1)S(1)}, s32[]{:S(2)}) async-start(s8[8192000]{0:T(1024)(128)(4,1)} %bitcast.41), calls=%async_computation.6 | async-start | bytes 8388608
  375.2 8.7 %copy-start.3 = (f32[32,5120]{1,0:T(8,128)}, f32[32,5120]{1,0:T(8,128)S(1)}, u32[]{:S(2)}) copy-start(f32[32,5120]{1,0:T(8,128)S(1)} %get-tuple-element.8) | copy-start | bytes 1966084
  375.3 8.7 %slice-start.1 = ((s8[8192000]{0:T(1024)(128)(4,1)}), s8[3997696]{0:T(1024)(128)(4,1)S(1)}, s32[]{:S(2)}) async-start(s8[8192000]{0:T(1024)(128)(4,1)} %bitcast.41), calls=%async_computation.7 | async-start | bytes 7995392
  386.5 197.9 %all-reduce.11.cloned.1.call-start = ((), (), s32[]{:S(2)}) async-start(), calls=%async_computation.5 | async-start | bytes 1310720 | tf_op jit(solution)/shard_map/psum | solution.py:72
  479.0 106.9 %copy-start.1 = (bf16[128,1600]{0,1:T(8,128)(2,1)S(1)}, bf16[128,1600]{0,1:T(8,128)(2,1)}, u32[]{:S(2)}) copy-start(bf16[128,1600]{0,1:T(8,128)(2,1)} %param.17) | copy-start | bytes 1228804
Sparse Core Ops, SparseCore 0:
  9.5 44.7 all-gather.4
  76.0 62.0 all-gather.2
  175.1 91.5 all-reduce.4
  282.5 90.8 all-reduce.6
  386.6 90.8 all-reduce.8
  493.4 90.8 all-reduce.10
where the time goes:
time: 595 us; the launch traced here: 593 us
  waiting for transfers between devices  354 us (59%)
  local copies, waits for them, and re-layouts  102 us (17%)
  matrix products  81 us (14%)
  blocking collectives  34.3 us (6%)
  between operations  13.7 us (2%)
  other arithmetic  7.34 us (1%)
    psum x4, waiting for transfers between devices, on_device(): lax.psum(jnp.dot(activated, merged_down, preferred_element_type=jnp.float...  353 us
    unnamed x25, local copies, waits for them, and re-layouts  81.9 us
    all_gather x1, blocking collectives, on_device(): lax.all_gather(down_a, 'fsdp', axis=1, tiled=True)  34.3 us
    dot_general x4, matrix products, on_device(): lax.dot_general(normed, merged_inputs, (((1,), (1,)), ((), ())), preferre...  34 us
    dot_general x4, matrix products, on_device(): jnp.dot(activated, merged_down, preferred_element_type=jnp.float32)  20 us
    slice x1, local copies, waits for them, and re-layouts, on_device(): stream = stream + looked[position].astype(jnp.float32)  17.8 us
  transfers between devices with their start and end apart: 6, of which 5 were waited for; matrix products, arithmetic and copies ran while one was open for 18% of the time, Pallas kernels for 0%

commit v1 on v0

v1 whole, which is shorter than its diff:
```python
import functools
import jax
import jax.numpy as jnp
from jax import lax
from jax.experimental import pallas as pl
from jax.experimental.pallas import tpu as pltpu
from jax.sharding import PartitionSpec as P

epsilon = 1e-06
bf16, f32 = jnp.bfloat16, jnp.float32
NT = (((1,), (1,)), ((), ()))
MESH = pl.DeviceIdType.MESH


def gather_kernel(ids_ref, table_ref, out_ref, blocks, placed, sems):
    count = blocks.shape[0]
    rows = table_ref.shape[0]

    def block_copy(i):
        start = pl.multiple_of((ids_ref[i] // 128) * 128, 128)
        return pltpu.make_async_copy(
            table_ref.at[:, pl.ds(start, 128)], blocks.at[i], sems.at[i]
        )

    def begin(i, carry):
        block_copy(i).start()
        return carry

    lax.fori_loop(0, count, begin, 0)
    placed[...] = jnp.zeros_like(placed)
    lane = lax.broadcasted_iota(jnp.int32, (rows, 128), 1)

    def place(i, carry):
        block_copy(i).wait()
        shift = lax.rem(i + 128 - lax.rem(ids_ref[i], 128), 128)
        turned = pltpu.roll(blocks[i].astype(f32), shift, 1)
        placed[:rows, :] = jnp.where(lane == i, turned, placed[:rows, :])
        return carry

    lax.fori_loop(0, count, place, 0)
    out = jnp.transpose(placed[...])[:, :rows].astype(bf16)
    out_ref[...] = out.reshape(out_ref.shape)


def gather_columns(token_ids, table):
    steps, rows = token_ids.shape
    count = steps * rows
    width = table.shape[0]
    padded = (width + 127) // 128 * 128
    return pl.pallas_call(
        gather_kernel,
        out_shape=jax.ShapeDtypeStruct((steps, 2, rows // 2, width), bf16),
        in_specs=[
            pl.BlockSpec(memory_space=pltpu.SMEM),
            pl.BlockSpec(memory_space=pl.ANY),
        ],
        out_specs=pl.BlockSpec(memory_space=pltpu.VMEM),
        scratch_shapes=[
            pltpu.VMEM((count, width, 128), bf16),
            pltpu.VMEM((padded, 128), f32),
            pltpu.SemaphoreType.DMA((count,)),
        ],
        compiler_params=pltpu.CompilerParams(vmem_limit_bytes=24 << 20),
        cost_estimate=pl.CostEstimate(
            flops=count * width * 128, bytes_accessed=count * width * 256, transcendentals=0
        ),
        name="embed_columns",
    )(token_ids.reshape(count), table)


def decode_kernel(
    F, X, looked_ref, gain_ref, gub_ref, gua_ref, dbt_ref, da_ref, gate_hbm, up_hbm, down_hbm,
    out_ref,
    wg, wu, wd, db, ag, stream, added, looked_in, acc_g, acc_u, act,
    sib_out, sib_in, own_part, rs_out, rs_in, fin_out, fin_in,
    w_sem, look_sem, ag_send, ag_recv, fw_send, fw_recv, sib_send, sib_recv, rs_send, rs_recv,
    fin_sem,
):
    S = looked_ref.shape[0]
    H = wg.shape[1]
    C = wg.shape[2]
    half = C // 2
    R = da_ref.shape[0]
    rows = 32
    Z = F // X
    grp = lax.axis_index("groups")
    me = lax.axis_index("fsdp")
    t = lax.axis_index("tensor")
    other = 1 - t
    z, x = me // X, me % X

    def ahead(k):
        return ((z + k // X) % Z) * X + (x + k % X) % X

    def behind(k):
        return ((z + Z - k // X) % Z) * X + (x + X - k % X) % X

    def w_copies(j, i):
        cols = pl.ds(pl.multiple_of(j * C, 128), C)
        return [
            pltpu.make_async_copy(h.at[:, cols], w.at[j], w_sem.at[n, i])
            for n, (h, w) in enumerate(((gate_hbm, wg), (up_hbm, wu), (down_hbm, wd)))
        ]

    for k in range(F):
        for c in w_copies(behind(k), k)[:2]:
            c.start()
    for i, k in enumerate(list(range(1, F)) + [0]):
        w_copies(ahead(k), i)[2].start()

    barrier = pltpu.get_barrier_semaphore()
    for k in range(1, F):
        pl.semaphore_signal(barrier, inc=1, device_id=(grp, ahead(k), t), device_id_type=MESH)
    pl.semaphore_signal(barrier, inc=1, device_id=(grp, me, other), device_id_type=MESH)
    pl.semaphore_wait(barrier, F)

    def remote(src, dst, ss, rs, dev):
        return pltpu.make_async_remote_copy(
            src_ref=src, dst_ref=dst, send_sem=ss, recv_sem=rs, device_id=dev, device_id_type=MESH
        )

    sibling = (grp, me, other)
    look = remote(looked_ref.at[:, other], looked_in, look_sem.at[0], look_sem.at[1], sibling)
    look.start()
    wide = dbt_ref[...]
    db[...] = jnp.where(t == 0, wide[:, :H].astype(f32), wide[:, H:].astype(f32)).astype(bf16)
    mine = looked_ref[:, t].astype(f32)
    look.wait()
    theirs = looked_in[...].astype(f32)
    for s in range(S):
        left = jnp.where(t == 0, mine[s], theirs[s])
        right = jnp.where(t == 0, theirs[s], mine[s])
        added[s] = jnp.concatenate([left, right], axis=1)
    stream[...] = jnp.zeros_like(stream)
    lane = lax.broadcasted_iota(jnp.int32, (rows, 2 * R), 1)

    def step(s, carry):
        now = stream[...] + added[s]
        stream[...] = now
        scaled = (now * gain_ref[pl.ds(me, 1), :]).astype(bf16)
        low = jnp.dot(scaled, gub_ref[...], preferred_element_type=f32)
        ag[s, me, t, :, :C] = now.astype(bf16)
        ag[s, me, t, :, C:] = low.astype(bf16)

        def ag_copy(j_from, k, dev):
            piece = ag.at[s, j_from, t]
            return remote(piece, piece, ag_send.at[k], ag_recv.at[s, j_from], dev)

        def fw_copy(j_from, k):
            piece = ag.at[s, j_from, t]
            return remote(piece, piece, fw_send.at[k], fw_recv.at[s, j_from], sibling)

        fw_copy(me, 0).start()
        for k in range(1, F):
            ag_copy(me, k, (grp, ahead(k), t)).start()

        squares = jnp.zeros((rows, 1), f32)
        lows = jnp.zeros((rows, 2 * R), f32)
        for k in range(F):
            if k + 1 < F:
                j_next = behind(k + 1)
                ag_copy(j_next, k + 1, (grp, j_next, t)).wait_recv()
                fw_copy(j_next, k + 1).start()
            j = behind(k)
            theirs_in = ag.at[s, j, other]
            remote(
                theirs_in, theirs_in, fw_send.at[k], fw_recv.at[s, j], sibling
            ).wait_recv()

            @pl.when(s == 0)
            def _():
                for c in w_copies(j, k)[:2]:
                    c.wait()

            piece = ag[s, j].reshape(rows, C + 2 * R)
            xs = piece[:, :C].astype(f32)
            squares += jnp.sum(xs * xs, axis=1, keepdims=True)
            lows += piece[:, C:].astype(f32)
            xn = (xs * gain_ref[pl.ds(j, 1), :]).astype(bf16)
            g = lax.dot_general(xn, wg[j], NT, preferred_element_type=f32)
            u = lax.dot_general(xn, wu[j], NT, preferred_element_type=f32)
            if k == 0:
                acc_g[...] = g
                acc_u[...] = u
            else:
                acc_g[...] += g
                acc_u[...] += u
        for k in range(1, F):
            ag_copy(me, k, (grp, ahead(k), t)).wait_send()
        for k in range(F):
            fw_copy(behind(k), k).wait_send()

        inverse_rms = lax.rsqrt(squares / (F * C) + epsilon)
        a_local = gua_ref[pl.ds(pl.multiple_of(t * H, 16), H), :]
        zero = jnp.zeros_like(lows)
        low_g = jnp.where(lane < R, lows, zero).astype(bf16)
        low_u = jnp.where(lane < R, zero, lows).astype(bf16)
        gate = acc_g[...] + lax.dot_general(low_g, a_local, NT, preferred_element_type=f32)
        up = acc_u[...] + lax.dot_general(low_u, a_local, NT, preferred_element_type=f32)
        gate = gate * inverse_rms
        up = up * inverse_rms
        act[...] = (gate / (1.0 + jnp.exp(-gate)) * up).astype(bf16)

        down_low = lax.dot_general(act[...], db[...], NT, preferred_element_type=f32)
        low_mine = jnp.where(t == 0, down_low[:16], down_low[16:])
        low_other = jnp.where(t == 0, down_low[16:], down_low[:16]).astype(bf16)

        def sib_copy(j):
            return remote(
                sib_out.at[j], sib_in.at[s, j], sib_send.at[j], sib_recv.at[s, j], sibling
            )

        def rs_copy(k):
            j = ahead(k)
            return remote(
                rs_out.at[j], rs_in.at[s, me], rs_send.at[k], rs_recv.at[s, me], (grp, j, t)
            )

        def finish(k):
            j = ahead(k)
            sib_copy(j).wait_recv()
            total = own_part[j] + sib_in[s, j].astype(f32)
            if k > 0:
                rs_out[j] = total.astype(bf16)
                rs_copy(k).start()
            return total

        order = list(range(1, F)) + [0]
        total = None
        for i, k in enumerate(order):
            j = ahead(k)

            @pl.when(s == 0)
            def _():
                w_copies(j, i)[2].wait()

            part = jnp.dot(act[...], wd[j], preferred_element_type=f32)
            own_part[j, :, :C] = jnp.where(t == 0, part[:16], part[16:])
            own_part[j, :, C:] = low_mine
            sib_out[j, :, :C] = jnp.where(t == 0, part[16:], part[:16]).astype(bf16)
            sib_out[j, :, C:] = low_other
            sib_copy(j).start()
            if i > 0:
                finish(order[i - 1])
        total = finish(0)
        for k in range(1, F):
            j = behind(k)
            remote(
                rs_out.at[j], rs_in.at[s, j], rs_send.at[k], rs_recv.at[s, j], (grp, j, t)
            ).wait_recv()
            total += rs_in[s, j].astype(f32)
        fix = jnp.dot(total[:, C:C + R].astype(bf16), da_ref[...], preferred_element_type=f32)
        stream[...] = stream[...] + total[:, :C] + fix
        for k in range(F):
            sib_copy(ahead(k)).wait_send()
            if k > 0:
                rs_copy(k).wait_send()
        return carry

    lax.fori_loop(0, S, step, 0)

    last = stream[...]
    keep = jnp.where(t == 0, last[:, :half], last[:, half:])
    fin_out[...] = jnp.where(t == 0, last[:, half:], last[:, :half]).astype(bf16)
    fin = remote(fin_out, fin_in, fin_sem.at[0], fin_sem.at[1], sibling)
    fin.start()
    out_ref[t] = keep.astype(bf16)
    fin.wait()
    out_ref[other] = fin_in[...]


def decode_steps(F, X, looked, gain, gub, gua_t, dbt, da, gate_base, up_base, down_base):
    S = looked.shape[0]
    H, D = gate_base.shape
    C = D // F
    R = da.shape[0]
    W = C + 2 * R
    vmem = pl.BlockSpec(memory_space=pltpu.VMEM)
    hbm = pl.BlockSpec(memory_space=pl.ANY)
    dma = pltpu.SemaphoreType.DMA
    return pl.pallas_call(
        functools.partial(decode_kernel, F, X),
        out_shape=jax.ShapeDtypeStruct((2, 16, C // 2), bf16),
        in_specs=[vmem] * 6 + [hbm] * 3,
        out_specs=vmem,
        scratch_shapes=[
            pltpu.VMEM((F, H, C), bf16),
            pltpu.VMEM((F, H, C), bf16),
            pltpu.VMEM((F, H, C), bf16),
            pltpu.VMEM((2 * R, H), bf16),
            pltpu.VMEM((S, F, 2, 16, W), bf16),
            pltpu.VMEM((16, C), f32),
            pltpu.VMEM((S, 16, C), f32),
            pltpu.VMEM((S, 16, C // 2), bf16),
            pltpu.VMEM((32, H), f32),
            pltpu.VMEM((32, H), f32),
            pltpu.VMEM((32, H), bf16),
            pltpu.VMEM((F, 16, W), bf16),
            pltpu.VMEM((S, F, 16, W), bf16),
            pltpu.VMEM((F, 16, W), f32),
            pltpu.VMEM((F, 16, W), bf16),
            pltpu.VMEM((S, F, 16, W), bf16),
            pltpu.VMEM((16, C // 2), bf16),
            pltpu.VMEM((16, C // 2), bf16),
            dma((3, F)),
            dma((2,)),
            dma((F,)),
            dma((S, F)),
            dma((F,)),
            dma((S, F)),
            dma((F,)),
            dma((S, F)),
            dma((F,)),
            dma((S, F)),
            dma((2,)),
        ],
        compiler_params=pltpu.CompilerParams(
            collective_id=0, has_side_effects=True, vmem_limit_bytes=52 << 20
        ),
        name="decode_steps",
    )(looked, gain, gub, gua_t, dbt, da, gate_base, up_base, down_base)


def on_device_kernels(
    x_chips, token_ids, embed_table, norm_gain, gate_base, up_base, down_base,
    gate_up_b, gate_up_a, down_b, down_a,
):
    F = lax.axis_size("fsdp")
    R = down_a.shape[0]
    looked = gather_columns(token_ids, embed_table)
    gain = norm_gain.astype(f32).reshape(F, -1)
    dbt = jnp.pad(down_b.T, ((0, R), (0, 0)))
    out = decode_steps(
        F, x_chips, looked, gain, gate_up_b, gate_up_a.T, dbt, down_a,
        gate_base, up_base, down_base,
    )
    return out.reshape(token_ids.shape[1], -1)


def on_device_plain(
    token_ids, embed_table, norm_gain, gate_base, up_base, down_base,
    gate_up_b, gate_up_a, down_b, down_a,
):
    tensor_slot = lax.axis_index("tensor")
    column_slot = lax.axis_index("fsdp") * lax.axis_size("tensor") + tensor_slot
    hidden_dev = gate_base.shape[0]
    columns_dev = embed_table.shape[0]
    rank_size = down_a.shape[0]
    model_width = gate_base.shape[1]
    rows_count = token_ids.shape[1]
    step_count = token_ids.shape[0]
    contract = (((0,), (1,)), ((), ()))
    narrow_local = lax.dynamic_slice_in_dim(gate_up_a, tensor_slot * hidden_dev, hidden_dev, 1)
    down_local = lax.dynamic_slice_in_dim(down_b, tensor_slot * hidden_dev, hidden_dev, 0)
    portion = lax.all_gather(gate_up_b, "fsdp", axis=0, tiled=True)
    gate_fix = lax.dot_general(
        narrow_local[:rank_size], portion[:, :rank_size], contract, preferred_element_type=f32
    )
    up_fix = lax.dot_general(
        narrow_local[rank_size:], portion[:, rank_size:], contract, preferred_element_type=f32
    )
    merged_inputs = jnp.concatenate(
        [
            (gate_base.astype(f32) + gate_fix).astype(bf16),
            (up_base.astype(f32) + up_fix).astype(bf16),
        ],
        axis=0,
    )
    down_fix = jnp.dot(
        down_local,
        lax.all_gather(down_a, "fsdp", axis=1, tiled=True),
        preferred_element_type=f32,
    )
    merged_down = (down_base.astype(f32) + down_fix).astype(bf16)
    looked_local = jnp.transpose(jnp.take(embed_table, token_ids, axis=1), (1, 2, 0))
    looked = lax.all_gather(looked_local, ("fsdp", "tensor"), axis=2, tiled=True)
    gain_value = norm_gain.astype(f32)
    stream = jnp.zeros((rows_count, model_width), f32)
    for position in range(step_count):
        stream = stream + looked[position].astype(f32)
        inverse_rms = lax.rsqrt(jnp.mean(stream * stream, axis=1, keepdims=True) + epsilon)
        normed = (stream * inverse_rms * gain_value).astype(bf16)
        preact = lax.dot_general(normed, merged_inputs, NT, preferred_element_type=f32)
        activated = (jax.nn.silu(preact[:, :hidden_dev]) * preact[:, hidden_dev:]).astype(bf16)
        stream = stream + lax.psum(
            jnp.dot(activated, merged_down, preferred_element_type=f32), ("fsdp", "tensor")
        )
    result = lax.dynamic_slice_in_dim(stream, column_slot * columns_dev, columns_dev, 1)
    return result.astype(bf16)


def solution(mesh):
    in_specs = (
        P(None, "groups"),
        P(("fsdp", "tensor"), None),
        P(),
        P(("fsdp", "tensor"), None),
        P(("fsdp", "tensor"), None),
        P(("fsdp", "tensor"), None),
        P("fsdp", None),
        P(None, "fsdp"),
        P("fsdp", None),
        P(None, "fsdp"),
    )
    out_specs = P("groups", ("fsdp", "tensor"))
    fits = mesh.shape["fsdp"] == 8 and mesh.shape["tensor"] == 2
    body = functools.partial(on_device_kernels, 2) if fits else on_device_plain
    return jax.shard_map(
        body, mesh=mesh, in_specs=in_specs, out_specs=out_specs, check_vma=False
    )
```

time: 595 us -> 107 us (0.18)
  waiting for transfers between devices: 354 us -> 0 us
  Pallas kernels: 0 us -> 105 us
  local copies, waits for them, and re-layouts: 102 us -> 2.16 us
  matrix products: 81 us -> 0 us
  blocking collectives: 34.3 us -> 0 us
  between operations: 13.7 us -> 0.09 us
  other arithmetic: 7.34 us -> 0 us
    psum x4 -> x0, waiting for transfers between devices: 353 us -> none  [on_device(): lax.psum(jnp.dot(activated, merged_down, preferred_element_type=jnp.float...]
    pallas_call x0 -> x2, Pallas kernels: none -> 105 us  [the longest x1 89 us: decode_steps(): pl.pallas_call(functools.partial(decode_kernel, F, X), out_shape=jax.Shap...]
    unnamed x25 -> x9, local copies, waits for them, and re-layouts: 81.9 us -> 0.64 us
    dot_general x11 -> x0, matrix products: 81 us -> none  [the longest x4 34 us: on_device(): lax.dot_general(normed, merged_inputs, (((1,), (1,)), ((), ())), preferre...]
    all_gather x1 -> x0, blocking collectives: 34.3 us -> none  [on_device(): lax.all_gather(down_a, 'fsdp', axis=1, tiled=True)]
    slice x1 -> x0, local copies, waits for them, and re-layouts: 17.8 us -> none  [on_device(): stream = stream + looked[position].astype(jnp.float32)]
  transfers between devices with their start and end apart: 6 -> 0, of which waited for: 5 -> 0; matrix products, arithmetic and copies ran while one was open for 18% -> 0% of each run, Pallas kernels for 0% -> 0%
where the time goes in v1:
time: 107 us
  Pallas kernels  105 us (98%)
  local copies, waits for them, and re-layouts  2.16 us (2%)
    pallas_call x1, Pallas kernels, decode_steps(): pl.pallas_call(functools.partial(decode_kernel, F, X), out_shape=jax.Shap...  89 us
    pallas_call x1, Pallas kernels, gather_columns(): pl.pallas_call(gather_kernel, out_shape=jax.ShapeDtypeStruct((steps, 2, r...  16 us

profile of v1, /device:TPU:0, one launch (start us, length us, event | category | flops | bytes accessed | tf_op | source)
XLA Modules:
  0.0 107.2 jit_solution(5611719156856234666)
XLA Ops:
  0.0 0.8 reshape.11.ids_ref
  0.8 0.7 reshape.16.gain_ref
  1.5 0.0 copy-start.3
  1.5 0.0 copy-start
  1.5 0.0 copy-start.1
  1.5 0.0 copy-start.2
  1.5 16.0 %embed_columns.1.looked_ref = bf16[4,2,16,320]{3,2,1,0:T(8,128)(2,1)S(1)} custom-call(s32[128]{0:T(128)S(1)} %reshape.11.ids_ref, bf16[320,76032]{1,0:T(8,128)(2,1)} %table_ref.1), custom_call_target="tpu_custom_call" | custom-call | flops 5242880 | bytes 10485760 | tf_op jit(solution)/shard_map/embed_columns/pallas_call | solution.py:50
  17.6 0.0 copy-done.3
  17.6 0.0 copy-done
  17.6 0.0 copy-done.1
  17.6 0.0 copy-done.2
  17.6 89.0 %decode_steps.1 = bf16[2,16,320]{2,1,0:T(8,128)(2,1)S(1)} custom-call(bf16[4,2,16,320]{3,2,1,0:T(8,128)(2,1)S(1)} %embed_columns.1.looked_ref, f32[8,640]{1,0:T(8,128)S(1)} %reshape.16.gain_ref, bf16[640,128]{1,0:T(8,128)(2,1)S(1)} %copy-done.1, bf16[1600,128]{1,0:T(8,128)(2,1)S(1)} %bitcast.3, bf16[128,1600]{1,0:T(8,128)(2,1)S(1)} %pad.4.dbt_ref, ...), custom_call_target="tpu_custom_call" | custom-call | tf_op jit(solution)/shard_map/decode_steps/pallas_call | solution.py:281
  106.6 0.6 copy.12
  (1 shorter events, 0.0 us)
Async XLA Ops:
  1.5 16.1 %copy-start.3 = (bf16[1600,64]{0,1:T(8,128)(2,1)S(1)}, bf16[1600,64]{0,1:T(8,128)(2,1)}, u32[]{:S(2)}) copy-start(bf16[1600,64]{0,1:T(8,128)(2,1)} %param.18) | copy-start | bytes 614404
  1.5 16.1 %copy-start = (bf16[128,1600]{0,1:T(8,128)(2,1)S(1)}, bf16[128,1600]{0,1:T(8,128)(2,1)}, u32[]{:S(2)}) copy-start(bf16[128,1600]{0,1:T(8,128)(2,1)} %param.17) | copy-start | bytes 1228804
  1.5 16.1 %copy-start.1 = (bf16[640,128]{1,0:T(8,128)(2,1)S(1)}, bf16[640,128]{1,0:T(8,128)(2,1)}, u32[]{:S(2)}) copy-start(bf16[640,128]{1,0:T(8,128)(2,1)} %gub_ref.1) | copy-start | bytes 491524
  1.5 16.1 %copy-start.2 = (bf16[64,640]{1,0:T(8,128)(2,1)S(1)}, bf16[64,640]{1,0:T(8,128)(2,1)}, u32[]{:S(2)}) copy-start(bf16[64,640]{1,0:T(8,128)(2,1)} %da_ref.1) | copy-start | bytes 245764

commit v2 on v1

--- a/solution.py
+++ b/solution.py
@@ -22,22 +22,32 @@
             table_ref.at[:, pl.ds(start, 128)], blocks.at[i], sems.at[i]
         )
 
+    unroll = 8
+
     def begin(i, carry):
-        block_copy(i).start()
+        for u in range(unroll):
+            block_copy(i * unroll + u).start()
         return carry
 
-    lax.fori_loop(0, count, begin, 0)
+    lax.fori_loop(0, count // unroll, begin, 0)
     placed[...] = jnp.zeros_like(placed)
-    lane = lax.broadcasted_iota(jnp.int32, (rows, 128), 1)
+    group = 64
+    lane = lax.broadcasted_iota(jnp.int32, (group, 128), 1)
 
     def place(i, carry):
-        block_copy(i).wait()
-        shift = lax.rem(i + 128 - lax.rem(ids_ref[i], 128), 128)
-        turned = pltpu.roll(blocks[i].astype(f32), shift, 1)
-        placed[:rows, :] = jnp.where(lane == i, turned, placed[:rows, :])
+        for u in range(unroll):
+            block_copy(i * unroll + u).wait()
+        for r in range(0, rows, group):
+            kept = placed[r:r + group, :]
+            for u in range(unroll):
+                token = i * unroll + u
+                shift = lax.rem(token + 128 - lax.rem(ids_ref[token], 128), 128)
+                turned = pltpu.roll(blocks[token, r:r + group].astype(f32), shift, 1)
+                kept = jnp.where(lane == token, turned, kept)
+            placed[r:r + group, :] = kept
         return carry
 
-    lax.fori_loop(0, count, place, 0)
+    lax.fori_loop(0, count // unroll, place, 0)
     out = jnp.transpose(placed[...])[:, :rows].astype(bf16)
     out_ref[...] = out.reshape(out_ref.shape)
 

time: 107 us -> 98.6 us (0.921)
  Pallas kernels: 105 us -> 96.1 us
    pallas_call x1, Pallas kernels: 16 us -> 7.16 us  [gather_columns(): pl.pallas_call(gather_kernel, out_shape=jax.ShapeDtypeStruct((steps, 2, r...]
where the time goes in v2:
time: 98.6 us; the launch traced here: 98.4 us
  Pallas kernels  96.1 us (97%)
  local copies, waits for them, and re-layouts  2.16 us (2%)
    pallas_call x1, Pallas kernels, decode_steps(): pl.pallas_call(functools.partial(decode_kernel, F, X), out_shape=jax.Shap...  89 us
    pallas_call x1, Pallas kernels, gather_columns(): pl.pallas_call(gather_kernel, out_shape=jax.ShapeDtypeStruct((steps, 2, r...  7.16 us

profile of v2, /device:TPU:0, one launch (start us, length us, event | category | flops | bytes accessed | tf_op | source)
XLA Modules:
  0.0 98.4 jit_solution(620328894807221495)
XLA Ops:
  0.0 0.8 reshape.11.ids_ref
  0.8 0.7 reshape.16.gain_ref
  1.5 0.0 copy-start.3
  1.5 0.0 copy-start
  1.5 0.0 copy-start.1
  1.5 0.0 copy-start.2
  1.5 7.2 %embed_columns.1.looked_ref = bf16[4,2,16,320]{3,2,1,0:T(8,128)(2,1)S(1)} custom-call(s32[128]{0:T(128)S(1)} %reshape.11.ids_ref, bf16[320,76032]{1,0:T(8,128)(2,1)} %table_ref.1), custom_call_target="tpu_custom_call" | custom-call | flops 5242880 | bytes 10485760 | tf_op jit(solution)/shard_map/embed_columns/pallas_call | solution.py:60
  8.7 0.0 copy-done.3
  8.8 0.0 copy-done
  8.8 0.0 copy-done.1
  8.8 0.0 copy-done.2
  8.8 89.0 %decode_steps.1 = bf16[2,16,320]{2,1,0:T(8,128)(2,1)S(1)} custom-call(bf16[4,2,16,320]{3,2,1,0:T(8,128)(2,1)S(1)} %embed_columns.1.looked_ref, f32[8,640]{1,0:T(8,128)S(1)} %reshape.16.gain_ref, bf16[640,128]{1,0:T(8,128)(2,1)S(1)} %copy-done.1, bf16[1600,128]{1,0:T(8,128)(2,1)S(1)} %bitcast.3, bf16[128,1600]{1,0:T(8,128)(2,1)S(1)} %pad.4.dbt_ref, ...), custom_call_target="tpu_custom_call" | custom-call | tf_op jit(solution)/shard_map/decode_steps/pallas_call | solution.py:291
  97.8 0.6 copy.12
  (1 shorter events, 0.0 us)
Async XLA Ops:
  1.5 7.2 %copy-start.3 = (bf16[1600,64]{0,1:T(8,128)(2,1)S(1)}, bf16[1600,64]{0,1:T(8,128)(2,1)}, u32[]{:S(2)}) copy-start(bf16[1600,64]{0,1:T(8,128)(2,1)} %param.18) | copy-start | bytes 614404
  1.5 7.3 %copy-start = (bf16[128,1600]{0,1:T(8,128)(2,1)S(1)}, bf16[128,1600]{0,1:T(8,128)(2,1)}, u32[]{:S(2)}) copy-start(bf16[128,1600]{0,1:T(8,128)(2,1)} %param.17) | copy-start | bytes 1228804
  1.5 7.3 %copy-start.1 = (bf16[640,128]{1,0:T(8,128)(2,1)S(1)}, bf16[640,128]{1,0:T(8,128)(2,1)}, u32[]{:S(2)}) copy-start(bf16[640,128]{1,0:T(8,128)(2,1)} %gub_ref.1) | copy-start | bytes 491524
  1.5 7.3 %copy-start.2 = (bf16[64,640]{1,0:T(8,128)(2,1)S(1)}, bf16[64,640]{1,0:T(8,128)(2,1)}, u32[]{:S(2)}) copy-start(bf16[64,640]{1,0:T(8,128)(2,1)} %da_ref.1) | copy-start | bytes 245764
